TPU v7x, 32 devices: a whole 2x2x4 slice. The times are simulated.
32 devices in a mesh: groups: 2 (over y), mem: 4 (over x, core), dp: 4 (over z).
Axes of the slice: x: 2, y: 2, z: 4, core: 2. Of those that a mesh axis runs over, the one named last changes fastest.
Arguments:
- queries: bfloat16 [8, 512, 1024], P(('groups', 'dp'), 'mem'), parts along dimension 0, may hold values from -6 to 6
- local_kv: bfloat16 [8, 512, 2, 1024], P(('groups', 'dp'), 'mem'), parts along dimension 0, may hold values from -9 to 9
- memory_kv: bfloat16 [8, 8, 8, 2, 64, 128], P(('groups', 'dp'), 'mem'), parts along dimension 0, may hold values from -9 to 9
- block_home: int32 [8, 8], P(('groups', 'dp')), parts along dimension 0, may hold values from 0 to 7, as said below
- retrieved: int32 [8, 1, 8, 16], P(('groups', 'dp')), parts along dimension 0, may hold values from -1 to 7, as said below
- stretch_pos: int32 [8, 1], P(('groups', 'dp')), parts along dimension 0, may hold values from 1 to 8, as said below
- gate_bias: float32 [8], replicated, may hold values from -2 to 2
- d_out: bfloat16 [8, 512, 1024], P(('groups', 'dp'), 'mem'), parts along dimension 0, may hold values from -12.5 to 12.5
Outputs:
- attended: bfloat16 [8, 512, 1024], P(('groups', 'dp'), 'mem'), parts along dimension 0
- grad_queries: bfloat16 [8, 512, 1024], P(('groups', 'dp'), 'mem'), parts along dimension 0
- grad_kv: bfloat16 [8, 512, 2, 1024], P(('groups', 'dp'), 'mem'), parts along dimension 0
- grad_gate: float32 [16], P('groups'), parts along dimension 0
There are 2 independent parts, one for each index of `groups`. A program takes and returns all parts, laid end to end along the dimension named above; an argument that names none is the same for every part. Nothing has to cross between parts.
Inputs may be any that keep to these rules, and one draw needn't show every extreme that they name: For each document a permutation: block r is stored in slot block_home[r] of memory_kv, which lies on index block_home[r] // 2 of mem. `retrieved`: each list names distinct blocks first and holds -1 after them. Of the named (block, head) entries of one stretch, at most 8 are stored on any one index of mem, and in each document one index of mem stores exactly 8 of every stretch's entries. Every list names a block below its stretch's stretch_pos. Block r is visible to stretch c when r < stretch_pos[c]; the last stretch of a document sees all 8 blocks.
All inputs are finite; a program needn't handle non-finite values.
Results may differ from a plain program's by a relative error of at most 0.012.
Values may be sent and summed in bfloat16 or wider, within the bound.
A program may use at most 64 MiB of HBM per device.

v0:
```python
import jax
import jax.numpy as jnp
from jax import lax
from jax.sharding import PartitionSpec as P

H = 8
HD = 128
TOK_DEV = 128
STRETCH = 512


neg_large = -1e30


def from_partner(block, axis, stride):
    count = lax.axis_size(axis)
    route = []
    for low in range(count):
        high = low | 1 << stride
        if high != low and high < count:
            route += [(low, high), (high, low)]
    return lax.ppermute(block, axis, route)


def masked_softmax(scores, visible):
    scores = jnp.where(visible, scores, neg_large)
    row_top = jnp.max(scores, axis=-1, keepdims=True)
    lifted = jnp.exp(scores - row_top)
    row_total = jnp.sum(lifted, axis=-1, keepdims=True)
    return lax.optimization_barrier((lifted / row_total).astype(jnp.bfloat16))


def fetch_blocks(memory_kv, slot_ids, head_ids):
    everything = lax.all_gather(memory_kv, "mem", axis=1, tiled=True)[0]
    return everything[slot_ids, head_ids]


def attend(query_heads, cotangent, fetched, visible, near_keys, near_vals, near_mask, gate_value):
    inv_sqrt = HD ** (-0.5)
    heads_here = fetched.shape[0]
    keys_n = fetched.shape[1] * fetched.shape[3]
    mem_keys = fetched[:, :, 0].reshape(heads_here, keys_n, HD)
    mem_vals = fetched[:, :, 1].reshape(heads_here, keys_n, HD)
    mem_mask = jnp.repeat(visible, fetched.shape[3], axis=1)[:, None, :]
    mem_scores = (
        jnp.einsum("qhd,hkd->hqk", query_heads, mem_keys, preferred_element_type=jnp.float32)
        * inv_sqrt
    )
    mem_probs = masked_softmax(mem_scores, mem_mask)
    mem_out = jnp.einsum("hqk,hkd->qhd", mem_probs, mem_vals, preferred_element_type=jnp.float32)
    near_scores = (
        jnp.einsum("qhd,khd->hqk", query_heads, near_keys, preferred_element_type=jnp.float32)
        * inv_sqrt
    )
    near_probs = masked_softmax(near_scores, near_mask)
    near_out = jnp.einsum("hqk,khd->qhd", near_probs, near_vals, preferred_element_type=jnp.float32)
    gate_col = gate_value[None, :, None]
    mixed = gate_col * mem_out + (1.0 - gate_col) * near_out
    mem_grad_out = gate_col * cotangent
    near_grad_out = (1.0 - gate_col) * cotangent
    gate_terms = (
        jnp.sum(cotangent * (mem_out - near_out), axis=(0, 2)) * gate_value * (1.0 - gate_value)
    )
    mem_delta = jnp.transpose(jnp.sum(mem_grad_out * mem_out, axis=2))[:, :, None]
    near_delta = jnp.transpose(jnp.sum(near_grad_out * near_out, axis=2))[:, :, None]
    mem_grad_low = mem_grad_out.astype(jnp.bfloat16)
    near_grad_low = near_grad_out.astype(jnp.bfloat16)
    mem_dprobs = jnp.einsum(
        "qhd,hkd->hqk", mem_grad_low, mem_vals, preferred_element_type=jnp.float32
    )
    mem_dscores = (mem_probs.astype(jnp.float32) * (mem_dprobs - mem_delta) * inv_sqrt).astype(
        jnp.bfloat16
    )
    near_dprobs = jnp.einsum(
        "qhd,khd->hqk", near_grad_low, near_vals, preferred_element_type=jnp.float32
    )
    near_dscores = (near_probs.astype(jnp.float32) * (near_dprobs - near_delta) * inv_sqrt).astype(
        jnp.bfloat16
    )
    query_grad = jnp.einsum(
        "hqk,hkd->qhd", mem_dscores, mem_keys, preferred_element_type=jnp.float32
    )
    query_grad = query_grad + jnp.einsum(
        "hqk,khd->qhd", near_dscores, near_keys, preferred_element_type=jnp.float32
    )
    return (mixed, query_grad, near_dscores, near_probs, near_grad_low, gate_terms)


def regroup(pieces):
    piece_count = pieces.shape[0]
    for bit_number in range(piece_count.bit_length() - 1):
        moving_rows = jnp.asarray(
            [k for k in range(piece_count) if k >> bit_number & 1], dtype=jnp.int32
        )
        arrived = from_partner(pieces[moving_rows], "mem", bit_number)
        pieces = pieces.at[moving_rows].set(arrived)
    return pieces


def per_device(queries, local_kv, memory_kv, block_home, retrieved, stretch_pos, gate_bias, d_out):
    my_index = lax.axis_index("mem")
    per_stretch = STRETCH // TOK_DEV
    rank_in_span = my_index % per_stretch
    stretch_index = my_index // per_stretch
    block_ids_all = lax.dynamic_index_in_dim(retrieved[0], stretch_index, 0, keepdims=False)
    stretch_limit = lax.dynamic_index_in_dim(stretch_pos[0], stretch_index, 0, keepdims=False)
    gate_value = jax.nn.sigmoid(gate_bias)
    head_group = H // per_stretch
    rank_order = rank_in_span ^ jnp.arange(per_stretch, dtype=jnp.int32)
    packed = jnp.concatenate(
        [
            queries[0].reshape(TOK_DEV, 1, H, HD),
            local_kv[0].reshape(TOK_DEV, 2, H, HD),
            d_out[0].reshape(TOK_DEV, 1, H, HD),
        ],
        axis=1,
    )
    by_rank = jnp.transpose(
        packed.reshape(TOK_DEV, 4, per_stretch, head_group, HD), (2, 0, 1, 3, 4)
    )
    gathered = regroup(by_rank[rank_order])[rank_order].reshape(STRETCH, 4, head_group, HD)
    query_heads = gathered[:, 0]
    first_head = rank_in_span * head_group
    head_ids = (first_head + jnp.arange(head_group, dtype=jnp.int32))[:, None]
    block_ids = lax.dynamic_slice_in_dim(block_ids_all, first_head, head_group, 0)
    visible = (block_ids >= 0) & (block_ids < stretch_limit)
    slot_ids = block_home[0][jnp.clip(block_ids, 0, block_home.shape[1] - 1)]
    fetched = fetch_blocks(memory_kv, slot_ids, head_ids)
    positions = jnp.arange(STRETCH, dtype=jnp.int32)
    near_mask = (positions[None, :] <= positions[:, None])[None]
    gate_mine = lax.dynamic_slice_in_dim(gate_value, first_head, head_group, 0)
    cotangent = gathered[:, 3].astype(jnp.float32)
    mixed, query_grad, near_dscores, near_probs, near_grad_low, gate_terms = attend(
        query_heads,
        cotangent,
        fetched,
        visible,
        gathered[:, 1],
        gathered[:, 2],
        near_mask,
        gate_mine,
    )
    ds_blocks = near_dscores.reshape(head_group, per_stretch, TOK_DEV, STRETCH)
    probs_blocks = near_probs.reshape(head_group, per_stretch, TOK_DEV, STRETCH)
    query_blocks = query_heads.reshape(per_stretch, TOK_DEV, head_group, HD)
    cot_blocks = near_grad_low.reshape(per_stretch, TOK_DEV, head_group, HD)
    key_terms = jnp.einsum(
        "hbqk,bqhd->bkhd", ds_blocks, query_blocks, preferred_element_type=jnp.float32
    ).astype(jnp.bfloat16)
    value_terms = jnp.einsum(
        "hbqk,bqhd->bkhd", probs_blocks, cot_blocks, preferred_element_type=jnp.float32
    ).astype(jnp.bfloat16)
    key_grad = jnp.sum(key_terms.astype(jnp.float32), axis=0).astype(jnp.bfloat16)
    value_grad = jnp.sum(value_terms.astype(jnp.float32), axis=0).astype(jnp.bfloat16)
    outgoing = jnp.stack(
        [mixed.astype(jnp.bfloat16), query_grad.astype(jnp.bfloat16), key_grad, value_grad], axis=1
    )
    outgoing = outgoing.reshape(per_stretch, TOK_DEV, 4, head_group, HD)
    returned = regroup(outgoing[rank_order])[rank_order]
    results = jnp.transpose(returned, (1, 2, 0, 3, 4)).reshape(TOK_DEV, 4, H * HD)
    attended = results[:, 0][None]
    grad_queries = results[:, 1][None]
    grad_kv = results[:, 2:4][None]
    gate_full = lax.dynamic_update_slice_in_dim(
        jnp.zeros((H,), jnp.float32), gate_terms, first_head, 0
    )
    grad_gate = lax.psum(gate_full, ("mem", "dp"))
    return (attended, grad_queries, grad_kv, grad_gate)


def solution(mesh):
    in_specs = (
        P(("groups", "dp"), "mem", None),
        P(("groups", "dp"), "mem", None, None),
        P(("groups", "dp"), "mem", None, None, None, None),
        P(("groups", "dp"), None),
        P(("groups", "dp"), None, None, None),
        P(("groups", "dp"), None),
        P(),
        P(("groups", "dp"), "mem", None),
    )
    out_specs = (
        P(("groups", "dp"), "mem", None),
        P(("groups", "dp"), "mem", None),
        P(("groups", "dp"), "mem", None, None),
        P("groups"),
    )
    return jax.shard_map(
        per_device, mesh=mesh, in_specs=in_specs, out_specs=out_specs, check_vma=False
    )
```

profile of v0, /device:TPU:0, one launch (start us, length us, event | category | flops | bytes accessed | tf_op | source)
XLA Modules:
  0.0 121.0 jit_solution(4376705952930379989)
XLA Ops:
  7.2 0.7 all-gather.2.cloned.1.call-update
  7.9 1.4 %copy.83 = bf16[1,128,2,1024]{1,3,2,0:T(8,128)(2,1)S(1)} copy(bf16[1,128,2,1024]{3,2,1,0:T(2,128)(2,1)} %param.13) | data formatting | bytes 1048576 | tf_op args[1]
  10.6 0.7 gather_fusion.2
  12.7 0.7 gather_fusion
  14.3 0.7 scatter_fusion
  15.7 2.7 %collective-permute-start.1 = (bf16[2,128,4,2,128]{4,1,3,2,0:T(8,128)(2,1)S(1)}, bf16[2,128,4,2,128]{4,1,3,2,0:T(8,128)(2,1)S(1)}, u32[]{:S(2)}, u32[]{:S(2)}) collective-permute-start(bf16[2,128,4,2,128]{4,1,3,2,0:T(8,128)(2,1)S(1)} %gather_fusion.4), channel_id=1, source_target_pairs={{0,8},{8,0},{4,12},{12,4},{1,9},{9,1},{5,13},{13,5},{2,10},{10,2},... | collective-permute-start | bytes 1572872 | tf_op jit(solution)/shard_map/ppermute | solution.py:22
  18.8 22.0 %collective-permute-done.1 = bf16[2,128,4,2,128]{4,1,3,2,0:T(8,128)(2,1)S(1)} collective-permute-done((bf16[2,128,4,2,128]{4,1,3,2,0:T(8,128)(2,1)S(1)}, bf16[2,128,4,2,128]{4,1,3,2,0:T(8,128)(2,1)S(1)}, u32[]{:S(2)}, u32[]{:S(2)}) %collective-permute-start.1) | collective-permute-done | bytes 524320 | tf_op jit(solution)/shard_map/ppermute | solution.py:22
  40.8 0.7 scatter_fusion.1
  41.6 0.7 gather_fusion.5
  42.4 2.2 %fusion.71 = (f32[2,512]{1,0:T(2,128)S(1)}, f32[2,512,512]{1,2,0:T(8,128)}) fusion(pred[512,512]{0,1:T(8,128)(4,1)S(1)} %iota_compare_fusion, bf16[512,4,2,128]{3,0,2,1:T(8,128)(2,1)S(1)} %bitcast.131), kind=kOutput, calls=%fused_computation.105 | convolution fusion | flops 136315392 | bytes 2887680 | tf_op jit(solution)/shard_map/sub | solution.py:28
  44.7 1.9 %divide_convert_fusion.1 = bf16[2,512,512]{1,2,0:T(8,128)(2,1)S(1)} fusion(f32[2,512,512]{1,2,0:T(8,128)} %get-tuple-element.29, f32[2,512]{1,0:T(2,128)S(1)} %get-tuple-element.28), kind=kLoop, calls=%fused_computation.22 | loop fusion | flops 1048576 | bytes 3149824 | tf_op jit(solution)/shard_map/convert_element_type | solution.py:30
  46.5 0.8 fusion.69
  48.2 2.3 %gather_fusion.1 = bf16[32,2,64,128]{3,2,1,0:T(8,128)(2,1)S(1)} fusion(bf16[8,8,2,64,128]{4,3,2,1,0:T(8,128)(2,1)} %bitcast.148, s32[32]{0:T(128)S(1)} %reshape.150), kind=kCustom, calls=%fused_computation.1 | custom fusion | bytes 2097408 | tf_op jit(solution)/shard_map/gather | solution.py:35
  50.6 0.9 fusion.70
  51.5 3.3 %fusion.74 = (f32[2,512]{1,0:T(2,128)S(1)}, f32[2,512,1024]{2,1,0:T(8,128)}) fusion(pred[2,1024]{1,0:T(4,128)(4,1)S(1)} %broadcast_in_dim.42, bf16[2,1024,128]{2,1,0:T(8,128)(2,1)S(1)} %bitcast.150, bf16[512,4,2,128]{3,0,2,1:T(8,128)(2,1)S(1)} %bitcast.133), kind=kOutput, calls=%fused_computation.106 | convolution fusion | flops 272630784 | bytes 4988928 | tf_op jit(solution)/shard_map/sub | solution.py:28
  54.8 2.8 %divide_convert_fusion = bf16[2,512,1024]{2,1,0:T(8,128)(2,1)S(1)} fusion(f32[2,512,1024]{2,1,0:T(8,128)} %get-tuple-element.31, f32[2,512]{1,0:T(2,128)S(1)} %get-tuple-element.30), kind=kLoop, calls=%fused_computation.17 | loop fusion | flops 2097152 | bytes 6295552 | tf_op jit(solution)/shard_map/convert_element_type | solution.py:30
  57.6 0.7 convolution_bitcast_fusion
  58.3 2.4 %fusion.19 = (f32[2]{0:T(128)S(1)}, f32[512,2]{0,1:T(2,128)S(1)}, f32[512,2]{0,1:T(2,128)S(1)}, bf16[512,2,128]{2,0,1:T(8,128)(2,1)}) fusion(f32[512,2,128]{2,0,1:T(8,128)S(1)} %convolution_bitcast_fusion, bf16[512,4,2,128]{3,0,2,1:T(8,128)(2,1)} %bitcast.134, f32[2]{0:T(128)S(1)} %get-tuple-element.19, f32[2]{0:T(128)S(1)} %get-tuple-element.20, ...), kind=kOutput, calls=%fused_computation.53 | convolution fusion | flops 136050688 | bytes 2367512 | tf_op jit(solution)/shard_map/hqk,khd->qhd/dot_general | solution.py:56
  60.7 3.7 %fusion.7 = f32[2,128,512]{2,1,0:T(8,128)} fusion(bf16[2,1024,128]{2,1,0:T(8,128)(2,1)} %bitcast.151, bf16[2,512,1024]{2,1,0:T(8,128)(2,1)S(1)} %divide_convert_fusion, bf16[2,1024,128]{2,1,0:T(8,128)(2,1)} %bitcast.140, f32[2,512]{1,0:T(2,128)S(1)} %bitcast.158, f32[2]{0:T(128)S(1)} %get-tuple-element.20, bf16[512,4,2,128]{3,0,2,1:T(8,128)(2,1)} %bitcast.135), kind=kOutput, calls=%fused_computation.29 | convolution fusion | flops 542507008 | bytes 3936264 | tf_op jit(solution)/shard_map/hqk,hkd->qhd/dot_general | solution.py:80
  64.4 1.6 %multiply_convert_fusion.1 = bf16[2,512,512]{1,2,0:T(8,128)(2,1)S(1)} fusion(bf16[2,512,512]{1,2,0:T(8,128)(2,1)S(1)} %divide_convert_fusion.1, f32[2,512]{1,0:T(2,128)S(1)} %bitcast.157, f32[2]{0:T(128)S(1)} %get-tuple-element.19, bf16[512,4,2,128]{3,0,2,1:T(8,128)(2,1)} %bitcast.136), kind=kOutput, calls=%fused_computation.21 | convolution fusion | flops 137232384 | bytes 2625544 | tf_op jit(solution)/shard_map/qhd,khd->hqk/dot_general | solution.py:74
  66.1 1.3 %fusion.11 = bf16[512,2,128]{0,2,1:T(8,128)(2,1)S(1)} fusion(f32[2,128,512]{2,1,0:T(8,128)S(1)} %copy-done.4, bf16[2,512,512]{1,2,0:T(8,128)(2,1)S(1)} %multiply_convert_fusion.1, bf16[512,4,2,128]{3,0,2,1:T(8,128)(2,1)} %bitcast.137), kind=kOutput, calls=%fused_computation.38 | convolution fusion | flops 134479872 | bytes 2097152 | tf_op jit(solution)/shard_map/hqk,khd->qhd/dot_general | solution.py:83
  68.4 0.7 gather_fusion.6
  69.9 1.9 %collective-permute-done.2 = bf16[2,128,4,2,128]{4,1,3,2,0:T(8,128)(2,1)S(1)} collective-permute-done((bf16[2,128,4,2,128]{4,1,3,2,0:T(8,128)(2,1)S(1)}, bf16[2,128,4,2,128]{4,1,3,2,0:T(8,128)(2,1)S(1)}, u32[]{:S(2)}, u32[]{:S(2)}) %collective-permute-start.2) | collective-permute-done | bytes 524320 | tf_op jit(solution)/shard_map/ppermute | solution.py:22
  71.8 0.7 scatter_fusion.2
  73.2 2.5 %collective-permute-start.3 = (bf16[2,128,4,2,128]{4,1,3,2,0:T(8,128)(2,1)S(1)}, bf16[2,128,4,2,128]{4,1,3,2,0:T(8,128)(2,1)S(1)}, u32[]{:S(2)}, u32[]{:S(2)}) collective-permute-start(bf16[2,128,4,2,128]{4,1,3,2,0:T(8,128)(2,1)S(1)} %gather_fusion.8), channel_id=1, source_target_pairs={{0,8},{8,0},{4,12},{12,4},{1,9},{9,1},{5,13},{13,5},{2,10},{10,2},... | collective-permute-start | bytes 1572872 | tf_op jit(solution)/shard_map/ppermute | solution.py:22
  75.9 33.2 %psum.7 = f32[8]{0:T(128)} all-reduce(f32[8]{0:T(128)S(1)} %multiply_dynamic-update-slice_fusion), channel_id=1, replica_groups=mesh['groups'=2,'mem'=4,'dp'=4] {'mem','dp'}, use_global_device_ids=true, to_apply=%region_13.14 | all-reduce | flops 8 | bytes 64 | tf_op jit(solution)/shard_map/psum | solution.py:167
  109.1 0.7 scatter_fusion.3
  109.8 0.7 gather_fusion.9
  110.6 0.7 copy.105
  111.3 1.1 copy.108
  112.5 0.9 copy.106
  113.3 0.9 copy.107
  (72 shorter events, 7.3 us)
Async XLA Ops:
  7.2 5.5 %copy-start = (s32[1,8]{1,0:T(1,128)S(1)}, s32[1,8]{1,0:T(1,128)}, u32[]{:S(2)}) copy-start(s32[1,8]{1,0:T(1,128)} %param.15) | copy-start | bytes 100
  7.2 2.5 %copy-start.6 = (bf16[1,128,1024]{2,1,0:T(8,128)(2,1)S(1)}, bf16[1,128,1024]{2,1,0:T(8,128)(2,1)}, u32[]{:S(2)}) copy-start(bf16[1,128,1024]{2,1,0:T(8,128)(2,1)} %param.12) | copy-start | bytes 786436
  7.2 2.8 %copy-start.7 = (bf16[1,128,1024]{2,1,0:T(8,128)(2,1)S(1)}, bf16[1,128,1024]{2,1,0:T(8,128)(2,1)}, u32[]{:S(2)}) copy-start(bf16[1,128,1024]{2,1,0:T(8,128)(2,1)} %param.19) | copy-start | bytes 786436
  7.2 41.0 %all-gather.2.cloned.1.call-start = ((), (), s32[]{:S(2)}) async-start(), calls=%async_computation | async-start | bytes 2621440 | tf_op jit(solution)/shard_map/all_gather | solution.py:34
  10.4 0.9 copy-start.10
  10.6 2.0 %copy-start.11 = (s32[1,1,8,16]{3,2,1,0:T(8,128)S(1)}, s32[1,1,8,16]{3,2,1,0:T(8,128)}, u32[]{:S(2)}) copy-start(s32[1,1,8,16]{3,2,1,0:T(8,128)} %param.16) | copy-start | bytes 1540
  10.6 3.7 %copy-start.9 = (s32[2]{0:T(128)S(1)}, s32[2]{0:T(128)}, u32[]{:S(2)}) copy-start(s32[2]{0:T(128)} %constant.103) | copy-start | bytes 28
  12.0 6.6 %copy-start.12 = (f32[8]{0:T(128)S(1)}, f32[8]{0:T(128)}, u32[]{:S(2)}) copy-start(f32[8]{0:T(128)} %param.18) | copy-start | bytes 100
  12.0 2.3 %collective-permute-start = (bf16[2,128,4,2,128]{4,1,3,2,0:T(8,128)(2,1)S(1)}, bf16[2,128,4,2,128]{4,1,3,2,0:T(8,128)(2,1)S(1)}, u32[]{:S(2)}, u32[]{:S(2)}) collective-permute-start(bf16[2,128,4,2,128]{4,1,3,2,0:T(8,128)(2,1)S(1)} %gather_fusion.3), channel_id=1, source_target_pairs={{0,4},{4,0},{8,12},{12,8},{1,5},{5,1},{9,13},{13,9},{2,6},{6,2},{1... | collective-permute-start | bytes 1572872 | tf_op jit(solution)/shard_map/ppermute | solution.py:22
  15.7 25.1 %collective-permute-start.1 = (bf16[2,128,4,2,128]{4,1,3,2,0:T(8,128)(2,1)S(1)}, bf16[2,128,4,2,128]{4,1,3,2,0:T(8,128)(2,1)S(1)}, u32[]{:S(2)}, u32[]{:S(2)}) collective-permute-start(bf16[2,128,4,2,128]{4,1,3,2,0:T(8,128)(2,1)S(1)} %gather_fusion.4), channel_id=1, source_target_pairs={{0,8},{8,0},{4,12},{12,4},{1,9},{9,1},{5,13},{13,5},{2,10},{10,2},... | collective-permute-start | bytes 1572872 | tf_op jit(solution)/shard_map/ppermute | solution.py:22
  42.4 9.1 %copy-start.1 = (bf16[4,128,4,2,128]{4,1,0,3,2:T(8,128)(2,1)}, bf16[4,128,4,2,128]{4,1,0,3,2:T(8,128)(2,1)S(1)}, u32[]{:S(2)}) copy-start(bf16[4,128,4,2,128]{4,1,0,3,2:T(8,128)(2,1)S(1)} %copy.88) | copy-start | bytes 3145732
  51.5 3.3 %copy-start.3 = (bf16[2,16,1,64,128]{4,3,1,0,2:T(8,128)(2,1)}, bf16[2,16,1,64,128]{4,3,1,0,2:T(8,128)(2,1)S(1)}, u32[]{:S(2)}) copy-start(bf16[2,16,1,64,128]{4,3,1,0,2:T(8,128)(2,1)S(1)} %get-tuple-element.27) | copy-start | bytes 1572868
  54.8 2.8 %copy-start.2 = (bf16[2,16,1,64,128]{4,3,1,0,2:T(8,128)(2,1)S(1)}, bf16[2,16,1,64,128]{4,3,1,0,2:T(8,128)(2,1)}, u32[]{:S(2)}) copy-start(bf16[2,16,1,64,128]{4,3,1,0,2:T(8,128)(2,1)} %get-tuple-element.26) | copy-start | bytes 1572868
  64.4 1.7 %copy-start.4 = (f32[2,128,512]{2,1,0:T(8,128)S(1)}, f32[2,128,512]{2,1,0:T(8,128)}, u32[]{:S(2)}) copy-start(f32[2,128,512]{2,1,0:T(8,128)} %fusion.7) | copy-start | bytes 1572868
  64.4 3.2 %copy-start.5 = (bf16[512,1,2,128]{3,0,2,1:T(8,128)(2,1)S(1)}, bf16[512,1,2,128]{3,0,2,1:T(8,128)(2,1)}, u32[]{:S(2)}) copy-start(bf16[512,1,2,128]{3,0,2,1:T(8,128)(2,1)} %get-tuple-element.24) | copy-start | bytes 786436
  66.1 2.2 %copy-start.8 = (bf16[512,2,128]{2,0,1:T(8,128)(2,1)S(1)}, bf16[512,2,128]{2,0,1:T(8,128)(2,1)}, u32[]{:S(2)}) copy-start(bf16[512,2,128]{2,0,1:T(8,128)(2,1)} %get-tuple-element.21) | copy-start | bytes 786436
  69.8 2.0 %collective-permute-start.2 = (bf16[2,128,4,2,128]{4,1,3,2,0:T(8,128)(2,1)S(1)}, bf16[2,128,4,2,128]{4,1,3,2,0:T(8,128)(2,1)S(1)}, u32[]{:S(2)}, u32[]{:S(2)}) collective-permute-start(bf16[2,128,4,2,128]{4,1,3,2,0:T(8,128)(2,1)S(1)} %gather_fusion.7), channel_id=1, source_target_pairs={{0,4},{4,0},{8,12},{12,8},{1,5},{5,1},{9,13},{13,9},{2,6},{6,2},{1... | collective-permute-start | bytes 1572872 | tf_op jit(solution)/shard_map/ppermute | solution.py:22
  73.2 35.8 %collective-permute-start.3 = (bf16[2,128,4,2,128]{4,1,3,2,0:T(8,128)(2,1)S(1)}, bf16[2,128,4,2,128]{4,1,3,2,0:T(8,128)(2,1)S(1)}, u32[]{:S(2)}, u32[]{:S(2)}) collective-permute-start(bf16[2,128,4,2,128]{4,1,3,2,0:T(8,128)(2,1)S(1)} %gather_fusion.8), channel_id=1, source_target_pairs={{0,8},{8,0},{4,12},{12,4},{1,9},{9,1},{5,13},{13,5},{2,10},{10,2},... | collective-permute-start | bytes 1572872 | tf_op jit(solution)/shard_map/ppermute | solution.py:22
Sparse Core Ops, SparseCore 0:
  9.6 33.9 all-gather.1
where the time goes:
time: 121 us
  blocking collectives  33.2 us (27%)
  waiting for transfers between devices  24.6 us (20%)
  local copies, waits for them, and re-layouts  19.8 us (16%)
  matrix products  16.2 us (13%)
  between operations  15.2 us (13%)
  other arithmetic  6.03 us (5%)
  starting transfers between devices  5.88 us (5%)
    psum x1, blocking collectives, per_device(): grad_gate = lax.psum(gate_full, ('mem', 'dp'))  33.2 us
    ppermute x4, waiting for transfers between devices, from_partner(): return lax.ppermute(block, axis, route)  23.9 us
    ppermute x4, starting transfers between devices, from_partner(): return lax.ppermute(block, axis, route)  5.85 us
    sub x2, matrix products, masked_softmax(): lifted = jnp.exp(scores - row_top)  5.54 us
    convert_element_type x2, other arithmetic, masked_softmax(): return lax.optimization_barrier((lifted / row_total).astype(jnp.bfloat16))  4.64 us
    dot_general x1, matrix products, attend(): jnp.einsum('hqk,hkd->qhd', mem_dscores, mem_keys, preferred_element_type=...  3.68 us
    scatter x4, local copies, waits for them, and re-layouts, regroup(): pieces = pieces.at[moving_rows].set(arrived)  2.98 us
    unnamed x30, local copies, waits for them, and re-layouts  2.91 us
  transfers between devices with their start and end apart: 5, of which 2 were waited for; matrix products, arithmetic and copies ran while one was open for 12% of the time, Pallas kernels for 0%

commit v1 on v0

--- a/solution.py
+++ b/solution.py
@@ -1,6 +1,10 @@
+import functools
+
 import jax
 import jax.numpy as jnp
 from jax import lax
+from jax.experimental import pallas as pl
+from jax.experimental.pallas import tpu as pltpu
 from jax.sharding import PartitionSpec as P
 
 H = 8
@@ -168,7 +172,393 @@
     return (attended, grad_queries, grad_kv, grad_gate)
 
 
+MESH_ID = pl.DeviceIdType.MESH
+SCALE = HD ** (-0.5)
+HG = H // 2
+
+
+def dot_nt(a, b):
+    return lax.dot_general(a, b, (((1,), (1,)), ((), ())), preferred_element_type=jnp.float32)
+
+
+def dot_tn(a, b):
+    return lax.dot_general(a, b, (((0,), (0,)), ((), ())), preferred_element_type=jnp.float32)
+
+
+def dot_nn(a, b):
+    return jnp.dot(a, b, preferred_element_type=jnp.float32)
+
+
+def probs_of(scores):
+    top = jnp.max(scores, axis=1, keepdims=True)
+    lifted = jnp.exp(scores - top)
+    return lifted * (1.0 / jnp.sum(lifted, axis=1, keepdims=True))
+
+
+def layer_kernel(
+    n_dp,
+    q_ref,
+    d_ref,
+    kv_ref,
+    mem_ref,
+    home_ref,
+    lists_ref,
+    limit_ref,
+    bias_ref,
+    att_ref,
+    dq_ref,
+    gkv_ref,
+    gate_ref,
+    qb,
+    db,
+    kvb,
+    memb,
+    mask_s,
+    att_s,
+    dq_s,
+    gkv_s,
+    gx_s,
+    gx,
+    gate_s,
+    gate_m,
+    gate_d,
+    send_sem,
+    recv_sem,
+    local_sem,
+):
+    me = lax.axis_index("mem")
+    dp = lax.axis_index("dp")
+    x = me // 2
+    c = me % 2
+    o = 1 - c
+    mate = 2 * x + o
+    far = 2 * (1 - x)
+    bf = jnp.bfloat16
+
+    def remote(src, dst, send_k, recv_k, device):
+        return pltpu.make_async_remote_copy(
+            src_ref=src,
+            dst_ref=dst,
+            send_sem=send_sem.at[send_k],
+            recv_sem=recv_sem.at[recv_k],
+            device_id=device,
+            device_id_type=MESH_ID,
+        )
+
+    def lanes(first, count):
+        return pl.ds(pl.multiple_of(first * HD, HD), count * HD)
+
+    barrier = pltpu.get_barrier_semaphore()
+    for k in range(1, 4):
+        pl.semaphore_signal(
+            barrier, inc=1, device_id={"mem": (me + k) % 4}, device_id_type=MESH_ID
+        )
+    for k in range(1, n_dp):
+        pl.semaphore_signal(
+            barrier, inc=1, device_id={"dp": (dp + k) % n_dp}, device_id_type=MESH_ID
+        )
+
+    locals_ = [
+        pltpu.make_async_copy(q_ref.at[:, lanes(c * HG, HG)], qb.at[c], local_sem.at[0]),
+        pltpu.make_async_copy(d_ref.at[:, lanes(c * HG, HG)], db.at[c], local_sem.at[1]),
+        pltpu.make_async_copy(kv_ref.at[pl.ds(c * HG, HG)], kvb.at[me], local_sem.at[2]),
+        pltpu.make_async_copy(mem_ref.at[:, pl.ds(c * HG, HG)], memb.at[me], local_sem.at[3]),
+    ]
+    for copy in locals_:
+        copy.start()
+
+    pl.semaphore_wait(barrier, 2 + n_dp)
+
+    core_copies = [
+        remote(q_ref.at[:, lanes(o * HG, HG)], qb.at[c], 0, 0, {"mem": mate}),
+        remote(d_ref.at[:, lanes(o * HG, HG)], db.at[c], 1, 1, {"mem": mate}),
+        remote(kv_ref.at[pl.ds(o * HG, HG)], kvb.at[me], 2, 2, {"mem": mate}),
+        remote(mem_ref.at[:, pl.ds(o * HG, HG)], memb.at[me], 3, 3, {"mem": mate}),
+    ]
+
+    def kv_copy(to, hh):
+        return remote(
+            kv_ref.at[to * HG + hh],
+            kvb.at[me, hh],
+            4 + to * HG + hh,
+            4 + c * HG + hh,
+            {"mem": far + to},
+        )
+
+    def mem_copy(to, hh):
+        return remote(
+            mem_ref.at[:, to * HG + hh],
+            memb.at[me, :, hh],
+            12 + to * HG + hh,
+            12 + c * HG + hh,
+            {"mem": far + to},
+        )
+
+    @pl.when(x == 0)
+    def _():
+        for hh in range(HG):
+            for to in range(2):
+                kv_copy(to, hh).start()
+            for to in range(2):
+                mem_copy(to, hh).start()
+
+    @pl.when(x == 1)
+    def _():
+        for hh in range(HG):
+            for to in range(2):
+                mem_copy(to, hh).start()
+
+    for copy in core_copies:
+        copy.start()
+
+    slots = 2 * 4
+    key_slot = lax.broadcasted_iota(jnp.int32, (H, slots * 64), 1) // 64
+    block_of = jnp.zeros((H, slots * 64), jnp.int32)
+    for r in range(slots):
+        block_of = jnp.where(key_slot == home_ref[0, r], r, block_of)
+    named = jnp.zeros((H, slots * 64), jnp.bool_)
+    for j in range(slots):
+        named = named | (block_of == lists_ref[0, 0, :, j : j + 1])
+    mask_s[...] = jnp.where(named & (block_of < limit_ref[0, 0]), 0.0, neg_large)
+    gate_s[...] = jnp.zeros_like(gate_s)
+
+    def res_copy(kind, hh):
+        head = c * HG + hh
+        if kind == 0:
+            return remote(
+                att_s.at[o, hh], att_ref.at[:, lanes(head, 1)], 20 + hh, 20 + hh, {"mem": mate}
+            )
+        if kind == 1:
+            return remote(
+                dq_s.at[o, hh], dq_ref.at[:, lanes(head, 1)], 24 + hh, 24 + hh, {"mem": mate}
+            )
+        return remote(gkv_s.at[o, hh], gkv_ref.at[head], 28 + hh, 28 + hh, {"mem": mate})
+
+    def gx_copy(to, hh):
+        return remote(
+            gx_s.at[to, hh],
+            gx.at[c * HG + hh],
+            32 + to * HG + hh,
+            32 + c * HG + hh,
+            {"mem": far + to},
+        )
+
+    def own_copy(kind, hh):
+        head = c * HG + hh
+        sem = local_sem.at[4 + kind * HG + hh]
+        if kind == 0:
+            return pltpu.make_async_copy(att_s.at[c, hh], att_ref.at[:, lanes(head, 1)], sem)
+        if kind == 1:
+            return pltpu.make_async_copy(dq_s.at[c, hh], dq_ref.at[:, lanes(head, 1)], sem)
+        return pltpu.make_async_copy(gkv_s.at[c, hh], gkv_ref.at[head], sem)
+
+    for copy in locals_:
+        copy.wait()
+    for copy in core_copies:
+        copy.wait_recv()
+
+    def one_head(hh, later):
+        rows = 2 * TOK_DEV
+        keys_n = 2 * TOK_DEV * (1 + later)
+        first = 0 if later else 0
+        head = c * HG + hh
+        query = qb[:, :, hh * HD : (hh + 1) * HD].reshape(rows, HD)
+        dout = db[:, :, hh * HD : (hh + 1) * HD].reshape(rows, HD).astype(jnp.float32)
+        near_keys = kvb[first : first + keys_n // TOK_DEV, hh, 0].reshape(keys_n, HD)
+        near_vals = kvb[first : first + keys_n // TOK_DEV, hh, 1].reshape(keys_n, HD)
+        mem_keys = memb[:, :, hh, 0].reshape(slots * 64, HD)
+        mem_vals = memb[:, :, hh, 1].reshape(slots * 64, HD)
+        gate = 1.0 / (1.0 + jnp.exp(-jnp.full((1, HD), bias_ref[head], jnp.float32)))
+        row = lax.broadcasted_iota(jnp.int32, (rows, keys_n), 0)
+        col = lax.broadcasted_iota(jnp.int32, (rows, keys_n), 1)
+        causal = col <= row + (keys_n - rows)
+        near_probs = probs_of(
+            jnp.where(causal, dot_nt(query, near_keys) * SCALE, neg_large)
+        )
+        near_low = near_probs.astype(bf)
+        near_out = dot_nn(near_low, near_vals)
+        mem_probs = probs_of(dot_nt(query, mem_keys) * SCALE + mask_s[pl.ds(head, 1), :])
+        mem_out = dot_nn(mem_probs.astype(bf), mem_vals)
+        mixed = (gate * mem_out + (1.0 - gate) * near_out).astype(bf)
+        att_s[:, hh] = mixed.reshape(2, TOK_DEV, HD)
+        gate_s[pl.ds(head, 1), :] = (
+            jnp.sum(dout * (mem_out - near_out), axis=0, keepdims=True) * gate * (1.0 - gate)
+        )
+        mem_cot = gate * dout
+        near_cot = (1.0 - gate) * dout
+        mem_delta = jnp.sum(mem_cot * mem_out, axis=1, keepdims=True)
+        near_delta = jnp.sum(near_cot * near_out, axis=1, keepdims=True)
+        near_cot16 = near_cot.astype(bf)
+        near_ds = (
+            near_probs * ((dot_nt(near_cot16, near_vals) - near_delta) * SCALE)
+        ).astype(bf)
+        key_grad = dot_tn(near_ds, query).astype(bf)
+        val_grad = dot_tn(near_low, near_cot16).astype(bf)
+        split = keys_n - rows
+        gkv_s[:, hh, 0] = key_grad[split:].reshape(2, TOK_DEV, HD)
+        gkv_s[:, hh, 1] = val_grad[split:].reshape(2, TOK_DEV, HD)
+        if later:
+            gx_s[:, hh, 0] = key_grad[:split].reshape(2, TOK_DEV, HD)
+            gx_s[:, hh, 1] = val_grad[:split].reshape(2, TOK_DEV, HD)
+            for to in range(2):
+                gx_copy(to, hh).start()
+        mem_ds = (
+            mem_probs * ((dot_nt(mem_cot.astype(bf), mem_vals) - mem_delta) * SCALE)
+        ).astype(bf)
+        query_grad = dot_nn(mem_ds, mem_keys) + dot_nn(near_ds, near_keys)
+        dq_s[:, hh] = query_grad.astype(bf).reshape(2, TOK_DEV, HD)
+        for kind in range(3):
+            res_copy(kind, hh).start()
+            own_copy(kind, hh).start()
+
+    @pl.when(x == 0)
+    def _():
+        for hh in range(HG):
+            for frm in range(2):
+                remote(
+                    mem_ref.at[:, 0], memb.at[2 + frm, :, hh], 0, 12 + frm * HG + hh, {"mem": mate}
+                ).wait_recv()
+            one_head(hh, False)
+
+    @pl.when(x == 1)
+    def _():
+        for hh in range(HG):
+            for frm in range(2):
+                remote(
+                    kv_ref.at[0], kvb.at[frm, hh], 0, 4 + frm * HG + hh, {"mem": mate}
+                ).wait_recv()
+                remote(
+                    mem_ref.at[:, 0], memb.at[frm, :, hh], 0, 12 + frm * HG + hh, {"mem": mate}
+                ).wait_recv()
+            one_head(hh, True)
+
+    gate_mem = [
+        remote(gate_s, gate_m.at[k - 1], 40 + k, 40 + k, {"mem": (me + k) % 4})
+        for k in range(1, 4)
+    ]
+    for copy in gate_mem:
+        copy.start()
+    for copy in gate_mem:
+        copy.wait()
+    gate_s2 = gate_d.at[0]
+    gate_s2[...] = gate_s[...] + gate_m[0] + gate_m[1] + gate_m[2]
+    gate_dp = [
+        remote(gate_s2, gate_d.at[k], 43 + k, 43 + k, {"dp": (dp + k) % n_dp})
+        for k in range(1, n_dp)
+    ]
+    for copy in gate_dp:
+        copy.start()
+
+    for kind in range(3):
+        for hh in range(HG):
+            own_copy(kind, hh).wait()
+            copy = res_copy(kind, hh)
+            copy.wait_send()
+    for hh in range(HG):
+        other = o * HG + hh
+        remote(
+            att_s.at[0, 0], att_ref.at[:, lanes(other, 1)], 0, 20 + hh, {"mem": mate}
+        ).wait_recv()
+        remote(
+            dq_s.at[0, 0], dq_ref.at[:, lanes(other, 1)], 0, 24 + hh, {"mem": mate}
+        ).wait_recv()
+        remote(gkv_s.at[0, 0], gkv_ref.at[other], 0, 28 + hh, {"mem": mate}).wait_recv()
+
+    @pl.when(x == 0)
+    def _():
+        for hh in range(HG):
+            for to in range(2):
+                kv_copy(to, hh).wait_send()
+        for hh in range(HG):
+            for frm in range(2):
+                head = frm * HG + hh
+                remote(
+                    gkv_s.at[0, 0], gx.at[head], 0, 32 + head, {"mem": mate}
+                ).wait_recv()
+                gkv_ref[head] = (
+                    gkv_ref[head].astype(jnp.float32) + gx[head].astype(jnp.float32)
+                ).astype(bf)
+
+    @pl.when(x == 1)
+    def _():
+        for hh in range(HG):
+            for to in range(2):
+                gx_copy(to, hh).wait_send()
+
+    for hh in range(HG):
+        for to in range(2):
+            mem_copy(to, hh).wait_send()
+    for copy in core_copies:
+        copy.wait_send()
+    for copy in gate_dp:
+        copy.wait()
+    total = gate_d[0]
+    for k in range(1, n_dp):
+        total = total + gate_d[k]
+    summed = jnp.broadcast_to(jnp.sum(total, axis=1, keepdims=True), (H, HD))
+    eye = lax.broadcasted_iota(jnp.int32, (H, HD), 0) == lax.broadcasted_iota(
+        jnp.int32, (H, HD), 1
+    )
+    gate_ref[...] = jnp.sum(jnp.where(eye, summed, 0.0), axis=0, keepdims=True)
+
+
+def one_stretch_per_document(
+    n_dp, queries, local_kv, memory_kv, block_home, retrieved, stretch_pos, gate_bias, d_out
+):
+    bf = jnp.bfloat16
+    kv_heads = jnp.transpose(local_kv.reshape(TOK_DEV, 2, H, HD), (2, 1, 0, 3))
+    vmem = pl.BlockSpec(memory_space=pltpu.VMEM)
+    smem = pl.BlockSpec(memory_space=pltpu.SMEM)
+    n_sems = 44 + n_dp
+    attended, grad_queries, grad_kv, grad_gate = pl.pallas_call(
+        functools.partial(layer_kernel, n_dp),
+        out_shape=(
+            jax.ShapeDtypeStruct((TOK_DEV, H * HD), bf),
+            jax.ShapeDtypeStruct((TOK_DEV, H * HD), bf),
+            jax.ShapeDtypeStruct((H, 2, TOK_DEV, HD), bf),
+            jax.ShapeDtypeStruct((1, HD), jnp.float32),
+        ),
+        in_specs=[vmem, vmem, vmem, vmem, smem, vmem, smem, smem],
+        out_specs=(vmem, vmem, vmem, vmem),
+        scratch_shapes=[
+            pltpu.VMEM((2, TOK_DEV, HG * HD), bf),
+            pltpu.VMEM((2, TOK_DEV, HG * HD), bf),
+            pltpu.VMEM((4, HG, 2, TOK_DEV, HD), bf),
+            pltpu.VMEM((4, 2, HG, 2, 64, HD), bf),
+            pltpu.VMEM((H, 512), jnp.float32),
+            pltpu.VMEM((2, HG, TOK_DEV, HD), bf),
+            pltpu.VMEM((2, HG, TOK_DEV, HD), bf),
+            pltpu.VMEM((2, HG, 2, TOK_DEV, HD), bf),
+            pltpu.VMEM((2, HG, 2, TOK_DEV, HD), bf),
+            pltpu.VMEM((H, 2, TOK_DEV, HD), bf),
+            pltpu.VMEM((H, HD), jnp.float32),
+            pltpu.VMEM((3, H, HD), jnp.float32),
+            pltpu.VMEM((n_dp, H, HD), jnp.float32),
+            pltpu.SemaphoreType.DMA((n_sems,)),
+            pltpu.SemaphoreType.DMA((n_sems,)),
+            pltpu.SemaphoreType.DMA((4 + 3 * HG,)),
+        ],
+        compiler_params=pltpu.CompilerParams(
+            collective_id=0, has_side_effects=True, vmem_limit_bytes=40 * 1024 * 1024
+        ),
+    )(
+        queries[0],
+        d_out[0],
+        kv_heads,
+        memory_kv[0],
+        block_home,
+        retrieved,
+        stretch_pos,
+        gate_bias,
+    )
+    grad_kv = jnp.transpose(grad_kv, (2, 1, 0, 3)).reshape(1, TOK_DEV, 2, H * HD)
+    return (attended[None], grad_queries[None], grad_kv, grad_gate[0, :H])
+
+
 def solution(mesh):
+    body = per_device
+    if mesh.shape["mem"] == STRETCH // TOK_DEV:
+        body = functools.partial(one_stretch_per_document, mesh.shape["dp"])
     in_specs = (
         P(("groups", "dp"), "mem", None),
         P(("groups", "dp"), "mem", None, None),
@@ -186,5 +576,5 @@
         P("groups"),
     )
     return jax.shard_map(
-        per_device, mesh=mesh, in_specs=in_specs, out_specs=out_specs, check_vma=False
-    )
+        body, mesh=mesh, in_specs=in_specs, out_specs=out_specs, check_vma=False
+    )

time: 121 us -> 47.7 us (0.39)
  Pallas kernels: 0 us -> 40.3 us
  blocking collectives: 33.2 us -> 0 us
  waiting for transfers between devices: 24.6 us -> 0 us
  matrix products: 16.2 us -> 0 us
  local copies, waits for them, and re-layouts: 19.8 us -> 5.84 us
  between operations: 15.2 us -> 1.36 us
  other arithmetic: 6.03 us -> 0 us
  starting transfers between devices: 5.88 us -> 0 us
    pallas_call x0 -> x1, Pallas kernels: none -> 40.3 us  [one_stretch_per_document(): pl.pallas_call(functools.partial(layer_kernel, n_dp), out_shape=(jax.Shap...]
    psum x1 -> x0, blocking collectives: 33.2 us -> none  [per_device(): grad_gate = lax.psum(gate_full, ('mem', 'dp'))]
    ppermute x4 -> x0, waiting for transfers between devices: 23.9 us -> none  [from_partner(): return lax.ppermute(block, axis, route)]
    dot_general x7 -> x0, matrix products: 10.7 us -> none  [the longest x1 3.68 us: attend(): jnp.einsum('hqk,hkd->qhd', mem_dscores, mem_keys, preferred_element_type=...]
    gather x13 -> x0, local copies, waits for them, and re-layouts: 8.9 us -> none  [the longest x4 2.59 us: regroup(): arrived = from_partner(pieces[moving_rows], 'mem', bit_number)]
    ppermute x4 -> x0, starting transfers between devices: 5.85 us -> none  [from_partner(): return lax.ppermute(block, axis, route)]
    sub x2 -> x0, matrix products: 5.54 us -> none  [masked_softmax(): lifted = jnp.exp(scores - row_top)]
    convert_element_type x2 -> x0, other arithmetic: 4.64 us -> none  [masked_softmax(): return lax.optimization_barrier((lifted / row_total).astype(jnp.bfloat16))]
  transfers between devices with their start and end apart: 5 -> 0, of which waited for: 2 -> 0; matrix products, arithmetic and copies ran while one was open for 12% -> 0% of each run, Pallas kernels for 0% -> 0%
where the time goes in v1:
time: 47.7 us; the launch traced here: 47.5 us
  Pallas kernels  40.3 us (84%)
  local copies, waits for them, and re-layouts  5.84 us (12%)
  between operations  1.36 us (3%)
    pallas_call x1, Pallas kernels, one_stretch_per_document(): pl.pallas_call(functools.partial(layer_kernel, n_dp), out_shape=(jax.Shap...  40.3 us
    unnamed x16, local copies, waits for them, and re-layouts  4.77 us

profile of v1, /device:TPU:0, one launch (start us, length us, event | category | flops | bytes accessed | tf_op | source)
XLA Modules:
  0.0 47.5 jit_solution(17508463828789572364)
XLA Ops:
  1.3 0.0 copy-start.3
  1.3 1.4 %copy.12 = bf16[1,128,2,1024]{1,3,2,0:T(8,128)(2,1)S(1)} copy(bf16[1,128,2,1024]{3,2,1,0:T(2,128)(2,1)} %param.9) | data formatting | bytes 1048576 | tf_op args[1]
  2.7 0.0 copy-start
  2.7 0.0 copy-start.1
  2.7 0.0 copy-start.2
  2.7 0.3 copy.13
  3.0 0.0 copy-start.4
  3.0 0.0 copy-start.5
  3.0 0.0 copy-done.3
  3.0 0.7 %copy-done = bf16[1,2,8,2,64,128]{5,4,3,2,1,0:T(8,128)(2,1)S(1)} copy-done((bf16[1,2,8,2,64,128]{5,4,3,2,1,0:T(8,128)(2,1)S(1)}, bf16[1,2,8,2,64,128]{5,4,3,2,1,0:T(8,128)(2,1)}, u32[]{:S(2)}) %copy-start) | copy-done | bytes 524312
  3.7 0.1 copy-done.1
  3.8 0.1 copy-done.2
  3.9 0.0 copy-done.4
  3.9 0.0 copy-done.5
  3.9 40.3 %shard_map.111 = (bf16[128,1024]{1,0:T(8,128)(2,1)S(1)}, bf16[128,1024]{1,0:T(8,128)(2,1)S(1)}, bf16[8,2,128,128]{3,2,1,0:T(8,128)(2,1)S(1)}, f32[1,128]{1,0:T(1,128)S(1)}) custom-call(bf16[128,1024]{1,0:T(8,128)(2,1)S(1)} %bitcast.14, bf16[128,1024]{1,0:T(8,128)(2,1)S(1)} %bitcast.15, bf16[8,2,128,128]{3,2,1,0:T(8,128)(2,1)S(1)} %bitcast.11, ...), custom_call_target="tpu_custom_call" | custom-call | tf_op jit(solution)/shard_map/pallas_call | solution.py:513
  44.2 0.5 %slice_bitcast_fusion = f32[8]{0:T(128)} fusion(f32[1,128]{1,0:T(1,128)S(1)} %get-tuple-element.11), kind=kLoop, calls=%fused_computation | loop fusion | bytes 64 | tf_op jit(solution)/shard_map/squeeze | solution.py:555
  44.7 0.3 copy.14
  45.0 1.1 %copy.15 = bf16[1,128,2,1024]{3,2,1,0:T(2,128)(2,1)} copy(bf16[1,128,2,1024]{1,3,2,0:T(8,128)(2,1)S(1)} %bitcast.18) | data formatting | bytes 1048576
  46.1 0.7 %copy.19 = bf16[1,128,1024]{2,1,0:T(8,128)(2,1)} copy(bf16[1,128,1024]{2,1,0:T(8,128)(2,1)S(1)} %bitcast.17) | data formatting | bytes 524288
  46.8 0.7 %copy.20 = bf16[1,128,1024]{2,1,0:T(8,128)(2,1)} copy(bf16[1,128,1024]{2,1,0:T(8,128)(2,1)S(1)} %bitcast.16) | data formatting | bytes 524288
Async XLA Ops:
  1.3 1.7 %copy-start.3 = (s32[1,1,8,16]{3,2,1,0:T(8,128)S(1)}, s32[1,1,8,16]{3,2,1,0:T(8,128)}, u32[]{:S(2)}) copy-start(s32[1,1,8,16]{3,2,1,0:T(8,128)} %lists_ref.1) | copy-start | bytes 1540
  2.7 1.0 %copy-start = (bf16[1,2,8,2,64,128]{5,4,3,2,1,0:T(8,128)(2,1)S(1)}, bf16[1,2,8,2,64,128]{5,4,3,2,1,0:T(8,128)(2,1)}, u32[]{:S(2)}) copy-start(bf16[1,2,8,2,64,128]{5,4,3,2,1,0:T(8,128)(2,1)} %param.10) | copy-start | bytes 1572868
  2.7 1.1 %copy-start.1 = (bf16[1,128,1024]{2,1,0:T(8,128)(2,1)S(1)}, bf16[1,128,1024]{2,1,0:T(8,128)(2,1)}, u32[]{:S(2)}) copy-start(bf16[1,128,1024]{2,1,0:T(8,128)(2,1)} %param.8) | copy-start | bytes 786436
  2.7 1.2 %copy-start.2 = (bf16[1,128,1024]{2,1,0:T(8,128)(2,1)S(1)}, bf16[1,128,1024]{2,1,0:T(8,128)(2,1)}, u32[]{:S(2)}) copy-start(bf16[1,128,1024]{2,1,0:T(8,128)(2,1)} %param.15) | copy-start | bytes 786436
  3.0 0.9 %copy-start.4 = (s32[1,8]{1,0:T(1,128)S(1)}, s32[1,8]{1,0:T(1,128)}, u32[]{:S(2)}) copy-start(s32[1,8]{1,0:T(1,128)} %home_ref.1) | copy-start | bytes 100
  3.0 0.9 %copy-start.5 = (f32[8]{0:T(128)S(1)}, f32[8]{0:T(128)}, u32[]{:S(2)}) copy-start(f32[8]{0:T(128)} %bias_ref.1) | copy-start | bytes 100

commit v2 on v1

--- a/solution.py
+++ b/solution.py
@@ -174,6 +174,7 @@
 
 MESH_ID = pl.DeviceIdType.MESH
 SCALE = HD ** (-0.5)
+CAP = 8
 HG = H // 2
 
 
@@ -203,6 +204,7 @@
     mem_ref,
     home_ref,
     lists_ref,
+    ids_ref,
     limit_ref,
     bias_ref,
     att_ref,
@@ -212,7 +214,8 @@
     qb,
     db,
     kvb,
-    memb,
+    mem_v,
+    packs,
     mask_s,
     att_s,
     dq_s,
@@ -262,10 +265,46 @@
         pltpu.make_async_copy(q_ref.at[:, lanes(c * HG, HG)], qb.at[c], local_sem.at[0]),
         pltpu.make_async_copy(d_ref.at[:, lanes(c * HG, HG)], db.at[c], local_sem.at[1]),
         pltpu.make_async_copy(kv_ref.at[pl.ds(c * HG, HG)], kvb.at[me], local_sem.at[2]),
-        pltpu.make_async_copy(mem_ref.at[:, pl.ds(c * HG, HG)], memb.at[me], local_sem.at[3]),
+        pltpu.make_async_copy(mem_ref, mem_v, local_sem.at[3]),
     ]
     for copy in locals_:
         copy.start()
+
+    slots = 2 * 4
+
+    def stored_flags(index):
+        flags = []
+        for low in range(2):
+            block = jnp.int32(0)
+            for r in range(slots):
+                block = jnp.where(home_ref[0, r] == 2 * index + low, r, block)
+            seen = block < limit_ref[0, 0]
+            for h in range(H):
+                found = ids_ref[0, 0, h, 0] == block
+                for j in range(1, slots):
+                    found = found | (ids_ref[0, 0, h, j] == block)
+                flags.append(jnp.where(found & seen, 1, 0))
+        return flags
+
+    def places(flags):
+        count = jnp.int32(0)
+        result = []
+        for flag in flags:
+            result.append(count)
+            count = count + flag
+        return result
+
+    mine = stored_flags(me)
+    mine_at = places(mine)
+    chosen = []
+    for k in range(CAP):
+        entry = jnp.int32(0)
+        for e in range(2 * H):
+            entry = jnp.where((mine[e] == 1) & (mine_at[e] == k), e, entry)
+        chosen.append(entry)
+    locals_[3].wait()
+    for k in range(CAP):
+        packs[me, k] = mem_v[chosen[k]]
 
     pl.semaphore_wait(barrier, 2 + n_dp)
 
@@ -273,7 +312,7 @@
         remote(q_ref.at[:, lanes(o * HG, HG)], qb.at[c], 0, 0, {"mem": mate}),
         remote(d_ref.at[:, lanes(o * HG, HG)], db.at[c], 1, 1, {"mem": mate}),
         remote(kv_ref.at[pl.ds(o * HG, HG)], kvb.at[me], 2, 2, {"mem": mate}),
-        remote(mem_ref.at[:, pl.ds(o * HG, HG)], memb.at[me], 3, 3, {"mem": mate}),
+        remote(packs.at[me], packs.at[me], 3, 3, {"mem": mate}),
     ]
 
     def kv_copy(to, hh):
@@ -285,33 +324,18 @@
             {"mem": far + to},
         )
 
-    def mem_copy(to, hh):
-        return remote(
-            mem_ref.at[:, to * HG + hh],
-            memb.at[me, :, hh],
-            12 + to * HG + hh,
-            12 + c * HG + hh,
-            {"mem": far + to},
-        )
+    pack_copy = remote(packs.at[me], packs.at[me], 12, 12, {"mem": far + c})
+    pack_copy.start()
 
     @pl.when(x == 0)
     def _():
         for hh in range(HG):
             for to in range(2):
                 kv_copy(to, hh).start()
-            for to in range(2):
-                mem_copy(to, hh).start()
-
-    @pl.when(x == 1)
-    def _():
-        for hh in range(HG):
-            for to in range(2):
-                mem_copy(to, hh).start()
 
     for copy in core_copies:
         copy.start()
 
-    slots = 2 * 4
     key_slot = lax.broadcasted_iota(jnp.int32, (H, slots * 64), 1) // 64
     block_of = jnp.zeros((H, slots * 64), jnp.int32)
     for r in range(slots):
@@ -352,23 +376,73 @@
             return pltpu.make_async_copy(dq_s.at[c, hh], dq_ref.at[:, lanes(head, 1)], sem)
         return pltpu.make_async_copy(gkv_s.at[c, hh], gkv_ref.at[head], sem)
 
-    for copy in locals_:
+    at = []
+    for index in range(4):
+        at.append([jnp.minimum(place, CAP - 1) for place in places(stored_flags(index))])
+
+    def entry_place(index, low, hh):
+        return jnp.where(c == 0, at[index][low * H + hh], at[index][low * H + HG + hh])
+
+    for copy in locals_[:3]:
         copy.wait()
     for copy in core_copies:
         copy.wait_recv()
+    pack_copy_in = remote(packs.at[me], packs.at[far + c], 12, 12, {"mem": mate})
+    pack_copy_in.wait_recv()
+    forward = remote(packs.at[far + c], packs.at[far + c], 13, 13, {"mem": mate})
+    forward.start()
+    remote(packs.at[me], packs.at[far + o], 13, 13, {"mem": mate}).wait_recv()
+
+    gate_mem = [
+        remote(gate_s, gate_m.at[k - 1], 40 + k, 40 + k, {"mem": (me + k) % 4})
+        for k in range(1, 4)
+    ]
+    gate_dp = [
+        remote(gate_d.at[0], gate_d.at[k], 43 + k, 43 + k, {"dp": (dp + k) % n_dp})
+        for k in range(1, n_dp)
+    ]
+
+    def gate_step():
+        for copy in gate_mem:
+            copy.wait()
+        gate_d[0] = gate_s[...] + gate_m[0] + gate_m[1] + gate_m[2]
+        for copy in gate_dp:
+            copy.start()
 
     def one_head(hh, later):
         rows = 2 * TOK_DEV
         keys_n = 2 * TOK_DEV * (1 + later)
-        first = 0 if later else 0
         head = c * HG + hh
         query = qb[:, :, hh * HD : (hh + 1) * HD].reshape(rows, HD)
         dout = db[:, :, hh * HD : (hh + 1) * HD].reshape(rows, HD).astype(jnp.float32)
-        near_keys = kvb[first : first + keys_n // TOK_DEV, hh, 0].reshape(keys_n, HD)
-        near_vals = kvb[first : first + keys_n // TOK_DEV, hh, 1].reshape(keys_n, HD)
-        mem_keys = memb[:, :, hh, 0].reshape(slots * 64, HD)
-        mem_vals = memb[:, :, hh, 1].reshape(slots * 64, HD)
         gate = 1.0 / (1.0 + jnp.exp(-jnp.full((1, HD), bias_ref[head], jnp.float32)))
+        mem_cot = gate * dout
+        near_cot = (1.0 - gate) * dout
+        near_cot16 = near_cot.astype(bf)
+
+        entries = [
+            packs[index, entry_place(index, low, hh)] for index in range(4) for low in range(2)
+        ]
+        mem_keys = jnp.concatenate([entry[0] for entry in entries], axis=0)
+        mem_vals = jnp.concatenate([entry[1] for entry in entries], axis=0)
+        mem_probs = probs_of(dot_nt(query, mem_keys) * SCALE + mask_s[pl.ds(head, 1), :])
+        mem_out = dot_nn(mem_probs.astype(bf), mem_vals)
+        mem_delta = jnp.sum(mem_cot * mem_out, axis=1, keepdims=True)
+        mem_ds = (
+            mem_probs * ((dot_nt(mem_cot.astype(bf), mem_vals) - mem_delta) * SCALE)
+        ).astype(bf)
+        query_grad = dot_nn(mem_ds, mem_keys)
+
+        if later:
+            for frm in range(2):
+                remote(
+                    kv_ref.at[0], kvb.at[frm, hh], 0, 4 + frm * HG + hh, {"mem": mate}
+                ).wait_recv()
+            near_keys = kvb[:, hh, 0].reshape(keys_n, HD)
+            near_vals = kvb[:, hh, 1].reshape(keys_n, HD)
+        else:
+            near_keys = kvb[0:2, hh, 0].reshape(keys_n, HD)
+            near_vals = kvb[0:2, hh, 1].reshape(keys_n, HD)
         row = lax.broadcasted_iota(jnp.int32, (rows, keys_n), 0)
         col = lax.broadcasted_iota(jnp.int32, (rows, keys_n), 1)
         causal = col <= row + (keys_n - rows)
@@ -377,35 +451,31 @@
         )
         near_low = near_probs.astype(bf)
         near_out = dot_nn(near_low, near_vals)
-        mem_probs = probs_of(dot_nt(query, mem_keys) * SCALE + mask_s[pl.ds(head, 1), :])
-        mem_out = dot_nn(mem_probs.astype(bf), mem_vals)
-        mixed = (gate * mem_out + (1.0 - gate) * near_out).astype(bf)
-        att_s[:, hh] = mixed.reshape(2, TOK_DEV, HD)
         gate_s[pl.ds(head, 1), :] = (
             jnp.sum(dout * (mem_out - near_out), axis=0, keepdims=True) * gate * (1.0 - gate)
         )
-        mem_cot = gate * dout
-        near_cot = (1.0 - gate) * dout
-        mem_delta = jnp.sum(mem_cot * mem_out, axis=1, keepdims=True)
+        if hh == HG - 1:
+            for copy in gate_mem:
+                copy.start()
         near_delta = jnp.sum(near_cot * near_out, axis=1, keepdims=True)
-        near_cot16 = near_cot.astype(bf)
         near_ds = (
             near_probs * ((dot_nt(near_cot16, near_vals) - near_delta) * SCALE)
         ).astype(bf)
         key_grad = dot_tn(near_ds, query).astype(bf)
         val_grad = dot_tn(near_low, near_cot16).astype(bf)
         split = keys_n - rows
-        gkv_s[:, hh, 0] = key_grad[split:].reshape(2, TOK_DEV, HD)
-        gkv_s[:, hh, 1] = val_grad[split:].reshape(2, TOK_DEV, HD)
         if later:
             gx_s[:, hh, 0] = key_grad[:split].reshape(2, TOK_DEV, HD)
             gx_s[:, hh, 1] = val_grad[:split].reshape(2, TOK_DEV, HD)
             for to in range(2):
                 gx_copy(to, hh).start()
-        mem_ds = (
-            mem_probs * ((dot_nt(mem_cot.astype(bf), mem_vals) - mem_delta) * SCALE)
-        ).astype(bf)
-        query_grad = dot_nn(mem_ds, mem_keys) + dot_nn(near_ds, near_keys)
+        gkv_s[:, hh, 0] = key_grad[split:].reshape(2, TOK_DEV, HD)
+        gkv_s[:, hh, 1] = val_grad[split:].reshape(2, TOK_DEV, HD)
+        mixed = (gate * mem_out + (1.0 - gate) * near_out).astype(bf)
+        att_s[:, hh] = mixed.reshape(2, TOK_DEV, HD)
+        if later and hh == HG - 1:
+            gate_step()
+        query_grad = query_grad + dot_nn(near_ds, near_keys)
         dq_s[:, hh] = query_grad.astype(bf).reshape(2, TOK_DEV, HD)
         for kind in range(3):
             res_copy(kind, hh).start()
@@ -414,40 +484,13 @@
     @pl.when(x == 0)
     def _():
         for hh in range(HG):
-            for frm in range(2):
-                remote(
-                    mem_ref.at[:, 0], memb.at[2 + frm, :, hh], 0, 12 + frm * HG + hh, {"mem": mate}
-                ).wait_recv()
             one_head(hh, False)
+        gate_step()
 
     @pl.when(x == 1)
     def _():
         for hh in range(HG):
-            for frm in range(2):
-                remote(
-                    kv_ref.at[0], kvb.at[frm, hh], 0, 4 + frm * HG + hh, {"mem": mate}
-                ).wait_recv()
-                remote(
-                    mem_ref.at[:, 0], memb.at[frm, :, hh], 0, 12 + frm * HG + hh, {"mem": mate}
-                ).wait_recv()
             one_head(hh, True)
-
-    gate_mem = [
-        remote(gate_s, gate_m.at[k - 1], 40 + k, 40 + k, {"mem": (me + k) % 4})
-        for k in range(1, 4)
-    ]
-    for copy in gate_mem:
-        copy.start()
-    for copy in gate_mem:
-        copy.wait()
-    gate_s2 = gate_d.at[0]
-    gate_s2[...] = gate_s[...] + gate_m[0] + gate_m[1] + gate_m[2]
-    gate_dp = [
-        remote(gate_s2, gate_d.at[k], 43 + k, 43 + k, {"dp": (dp + k) % n_dp})
-        for k in range(1, n_dp)
-    ]
-    for copy in gate_dp:
-        copy.start()
 
     for kind in range(3):
         for hh in range(HG):
@@ -485,9 +528,8 @@
             for to in range(2):
                 gx_copy(to, hh).wait_send()
 
-    for hh in range(HG):
-        for to in range(2):
-            mem_copy(to, hh).wait_send()
+    pack_copy.wait_send()
+    forward.wait_send()
     for copy in core_copies:
         copy.wait_send()
     for copy in gate_dp:
@@ -509,6 +551,7 @@
     kv_heads = jnp.transpose(local_kv.reshape(TOK_DEV, 2, H, HD), (2, 1, 0, 3))
     vmem = pl.BlockSpec(memory_space=pltpu.VMEM)
     smem = pl.BlockSpec(memory_space=pltpu.SMEM)
+    hbm = pl.BlockSpec(memory_space=pl.ANY)
     n_sems = 44 + n_dp
     attended, grad_queries, grad_kv, grad_gate = pl.pallas_call(
         functools.partial(layer_kernel, n_dp),
@@ -518,13 +561,14 @@
             jax.ShapeDtypeStruct((H, 2, TOK_DEV, HD), bf),
             jax.ShapeDtypeStruct((1, HD), jnp.float32),
         ),
-        in_specs=[vmem, vmem, vmem, vmem, smem, vmem, smem, smem],
+        in_specs=[hbm, hbm, vmem, hbm, smem, vmem, smem, smem, smem],
         out_specs=(vmem, vmem, vmem, vmem),
         scratch_shapes=[
             pltpu.VMEM((2, TOK_DEV, HG * HD), bf),
             pltpu.VMEM((2, TOK_DEV, HG * HD), bf),
             pltpu.VMEM((4, HG, 2, TOK_DEV, HD), bf),
-            pltpu.VMEM((4, 2, HG, 2, 64, HD), bf),
+            pltpu.VMEM((2 * H, 2, 64, HD), bf),
+            pltpu.VMEM((4, CAP, 2, 64, HD), bf),
             pltpu.VMEM((H, 512), jnp.float32),
             pltpu.VMEM((2, HG, TOK_DEV, HD), bf),
             pltpu.VMEM((2, HG, TOK_DEV, HD), bf),
@@ -545,8 +589,9 @@
         queries[0],
         d_out[0],
         kv_heads,
-        memory_kv[0],
+        memory_kv[0].reshape(2 * H, 2, 64, HD),
         block_home,
+        retrieved,
         retrieved,
         stretch_pos,
         gate_bias,

time: 47.7 us -> 38.8 us (0.81)
  Pallas kernels: 40.3 us -> 31.5 us
    pallas_call x1, Pallas kernels: 40.3 us -> 31.5 us  [one_stretch_per_document(): pl.pallas_call(functools.partial(layer_kernel, n_dp), out_shape=(jax.Shap...]
where the time goes in v2:
time: 38.8 us; the launch traced here: 38.7 us
  Pallas kernels  31.5 us (81%)
  local copies, waits for them, and re-layouts  5.84 us (15%)
  between operations  1.36 us (4%)
    pallas_call x1, Pallas kernels, one_stretch_per_document(): pl.pallas_call(functools.partial(layer_kernel, n_dp), out_shape=(jax.Shap...  31.5 us
    unnamed x16, local copies, waits for them, and re-layouts  4.77 us

profile of v2, /device:TPU:0, one launch (start us, length us, event | category | flops | bytes accessed | tf_op | source)
XLA Modules:
  0.0 38.7 jit_solution(5442629712478678302)
XLA Ops:
  1.3 0.0 copy-start.3
  1.3 1.4 %copy.12 = bf16[1,128,2,1024]{1,3,2,0:T(8,128)(2,1)S(1)} copy(bf16[1,128,2,1024]{3,2,1,0:T(2,128)(2,1)} %param.9) | data formatting | bytes 1048576 | tf_op args[1]
  2.7 0.0 copy-start
  2.7 0.0 copy-start.1
  2.7 0.0 copy-start.2
  2.7 0.3 copy.13
  3.0 0.0 copy-start.4
  3.0 0.0 copy-start.5
  3.0 0.0 copy-done.3
  3.0 0.7 %copy-done = bf16[1,2,8,2,64,128]{5,4,3,2,1,0:T(8,128)(2,1)S(1)} copy-done((bf16[1,2,8,2,64,128]{5,4,3,2,1,0:T(8,128)(2,1)S(1)}, bf16[1,2,8,2,64,128]{5,4,3,2,1,0:T(8,128)(2,1)}, u32[]{:S(2)}) %copy-start) | copy-done | bytes 524312
  3.7 0.1 copy-done.1
  3.8 0.1 copy-done.2
  3.9 0.0 copy-done.4
  3.9 0.0 copy-done.5
  3.9 31.5 %shard_map.111 = (bf16[128,1024]{1,0:T(8,128)(2,1)S(1)}, bf16[128,1024]{1,0:T(8,128)(2,1)S(1)}, bf16[8,2,128,128]{3,2,1,0:T(8,128)(2,1)S(1)}, f32[1,128]{1,0:T(1,128)S(1)}) custom-call(bf16[128,1024]{1,0:T(8,128)(2,1)S(1)} %bitcast.14, bf16[128,1024]{1,0:T(8,128)(2,1)S(1)} %bitcast.15, bf16[8,2,128,128]{3,2,1,0:T(8,128)(2,1)S(1)} %bitcast.11, ...), custom_call_target="tpu_custom_call" | custom-call | tf_op jit(solution)/shard_map/pallas_call | solution.py:556
  35.3 0.5 %slice_bitcast_fusion = f32[8]{0:T(128)} fusion(f32[1,128]{1,0:T(1,128)S(1)} %get-tuple-element.11), kind=kLoop, calls=%fused_computation | loop fusion | bytes 64 | tf_op jit(solution)/shard_map/squeeze | solution.py:600
  35.9 0.3 copy.14
  36.1 1.1 %copy.15 = bf16[1,128,2,1024]{3,2,1,0:T(2,128)(2,1)} copy(bf16[1,128,2,1024]{1,3,2,0:T(8,128)(2,1)S(1)} %bitcast.18) | data formatting | bytes 1048576
  37.3 0.7 %copy.19 = bf16[1,128,1024]{2,1,0:T(8,128)(2,1)} copy(bf16[1,128,1024]{2,1,0:T(8,128)(2,1)S(1)} %bitcast.17) | data formatting | bytes 524288
  38.0 0.7 %copy.20 = bf16[1,128,1024]{2,1,0:T(8,128)(2,1)} copy(bf16[1,128,1024]{2,1,0:T(8,128)(2,1)S(1)} %bitcast.16) | data formatting | bytes 524288
Async XLA Ops:
  1.3 1.7 %copy-start.3 = (s32[1,1,8,16]{3,2,1,0:T(8,128)S(1)}, s32[1,1,8,16]{3,2,1,0:T(8,128)}, u32[]{:S(2)}) copy-start(s32[1,1,8,16]{3,2,1,0:T(8,128)} %ids_ref.1) | copy-start | bytes 1540
  2.7 1.0 %copy-start = (bf16[1,2,8,2,64,128]{5,4,3,2,1,0:T(8,128)(2,1)S(1)}, bf16[1,2,8,2,64,128]{5,4,3,2,1,0:T(8,128)(2,1)}, u32[]{:S(2)}) copy-start(bf16[1,2,8,2,64,128]{5,4,3,2,1,0:T(8,128)(2,1)} %param.10) | copy-start | bytes 1572868
  2.7 1.1 %copy-start.1 = (bf16[1,128,1024]{2,1,0:T(8,128)(2,1)S(1)}, bf16[1,128,1024]{2,1,0:T(8,128)(2,1)}, u32[]{:S(2)}) copy-start(bf16[1,128,1024]{2,1,0:T(8,128)(2,1)} %param.8) | copy-start | bytes 786436
  2.7 1.2 %copy-start.2 = (bf16[1,128,1024]{2,1,0:T(8,128)(2,1)S(1)}, bf16[1,128,1024]{2,1,0:T(8,128)(2,1)}, u32[]{:S(2)}) copy-start(bf16[1,128,1024]{2,1,0:T(8,128)(2,1)} %param.15) | copy-start | bytes 786436
  3.0 0.9 %copy-start.4 = (s32[1,8]{1,0:T(1,128)S(1)}, s32[1,8]{1,0:T(1,128)}, u32[]{:S(2)}) copy-start(s32[1,8]{1,0:T(1,128)} %home_ref.1) | copy-start | bytes 100
  3.0 0.9 %copy-start.5 = (f32[8]{0:T(128)S(1)}, f32[8]{0:T(128)}, u32[]{:S(2)}) copy-start(f32[8]{0:T(128)} %bias_ref.1) | copy-start | bytes 100

commit v3 on v2

--- a/solution.py
+++ b/solution.py
@@ -209,8 +209,9 @@
     bias_ref,
     att_ref,
     dq_ref,
-    gkv_ref,
+    gint_ref,
     gate_ref,
+    gkv_v,
     qb,
     db,
     kvb,
@@ -324,6 +325,8 @@
             {"mem": far + to},
         )
 
+    for copy in core_copies[:3]:
+        copy.start()
     pack_copy = remote(packs.at[me], packs.at[me], 12, 12, {"mem": far + c})
     pack_copy.start()
 
@@ -333,8 +336,7 @@
             for to in range(2):
                 kv_copy(to, hh).start()
 
-    for copy in core_copies:
-        copy.start()
+    core_copies[3].start()
 
     key_slot = lax.broadcasted_iota(jnp.int32, (H, slots * 64), 1) // 64
     block_of = jnp.zeros((H, slots * 64), jnp.int32)
@@ -356,7 +358,7 @@
             return remote(
                 dq_s.at[o, hh], dq_ref.at[:, lanes(head, 1)], 24 + hh, 24 + hh, {"mem": mate}
             )
-        return remote(gkv_s.at[o, hh], gkv_ref.at[head], 28 + hh, 28 + hh, {"mem": mate})
+        return remote(gkv_s.at[o, hh], gkv_v.at[head], 28 + hh, 28 + hh, {"mem": mate})
 
     def gx_copy(to, hh):
         return remote(
@@ -374,7 +376,7 @@
             return pltpu.make_async_copy(att_s.at[c, hh], att_ref.at[:, lanes(head, 1)], sem)
         if kind == 1:
             return pltpu.make_async_copy(dq_s.at[c, hh], dq_ref.at[:, lanes(head, 1)], sem)
-        return pltpu.make_async_copy(gkv_s.at[c, hh], gkv_ref.at[head], sem)
+        return pltpu.make_async_copy(gkv_s.at[c, hh], gkv_v.at[head], sem)
 
     at = []
     for index in range(4):
@@ -505,7 +507,10 @@
         remote(
             dq_s.at[0, 0], dq_ref.at[:, lanes(other, 1)], 0, 24 + hh, {"mem": mate}
         ).wait_recv()
-        remote(gkv_s.at[0, 0], gkv_ref.at[other], 0, 28 + hh, {"mem": mate}).wait_recv()
+        remote(gkv_s.at[0, 0], gkv_v.at[other], 0, 28 + hh, {"mem": mate}).wait_recv()
+
+    def join_pairs(head, both):
+        gint_ref[:, :, head * HD : (head + 1) * HD] = jnp.stack([both[0], both[1]], axis=1)
 
     @pl.when(x == 0)
     def _():
@@ -518,12 +523,13 @@
                 remote(
                     gkv_s.at[0, 0], gx.at[head], 0, 32 + head, {"mem": mate}
                 ).wait_recv()
-                gkv_ref[head] = (
-                    gkv_ref[head].astype(jnp.float32) + gx[head].astype(jnp.float32)
-                ).astype(bf)
+                both = gkv_v[head].astype(jnp.float32) + gx[head].astype(jnp.float32)
+                join_pairs(head, both.astype(bf))
 
     @pl.when(x == 1)
     def _():
+        for head in range(H):
+            join_pairs(head, gkv_v[head])
         for hh in range(HG):
             for to in range(2):
                 gx_copy(to, hh).wait_send()
@@ -558,12 +564,13 @@
         out_shape=(
             jax.ShapeDtypeStruct((TOK_DEV, H * HD), bf),
             jax.ShapeDtypeStruct((TOK_DEV, H * HD), bf),
-            jax.ShapeDtypeStruct((H, 2, TOK_DEV, HD), bf),
+            jax.ShapeDtypeStruct((TOK_DEV, 2, H * HD), bf),
             jax.ShapeDtypeStruct((1, HD), jnp.float32),
         ),
         in_specs=[hbm, hbm, vmem, hbm, smem, vmem, smem, smem, smem],
         out_specs=(vmem, vmem, vmem, vmem),
         scratch_shapes=[
+            pltpu.VMEM((H, 2, TOK_DEV, HD), bf),
             pltpu.VMEM((2, TOK_DEV, HG * HD), bf),
             pltpu.VMEM((2, TOK_DEV, HG * HD), bf),
             pltpu.VMEM((4, HG, 2, TOK_DEV, HD), bf),
@@ -596,8 +603,7 @@
         stretch_pos,
         gate_bias,
     )
-    grad_kv = jnp.transpose(grad_kv, (2, 1, 0, 3)).reshape(1, TOK_DEV, 2, H * HD)
-    return (attended[None], grad_queries[None], grad_kv, grad_gate[0, :H])
+    return (attended[None], grad_queries[None], grad_kv[None], grad_gate[0, :H])
 
 
 def solution(mesh):

time: 38.8 us -> 38.2 us (0.985)
  local copies, waits for them, and re-layouts: 5.84 us -> 5.26 us
where the time goes in v3:
time: 38.2 us; the launch traced here: 38.1 us
  Pallas kernels  31.5 us (82%)
  local copies, waits for them, and re-layouts  5.26 us (14%)
  between operations  1.36 us (4%)
    pallas_call x1, Pallas kernels, one_stretch_per_document(): pl.pallas_call(functools.partial(layer_kernel, n_dp), out_shape=(jax.Shap...  31.5 us
    unnamed x16, local copies, waits for them, and re-layouts  4.46 us

profile of v3, /device:TPU:0, one launch (start us, length us, event | category | flops | bytes accessed | tf_op | source)
XLA Modules:
  0.0 38.1 jit_solution(5878182060581224279)
XLA Ops:
  1.3 0.0 copy-start.3
  1.3 1.4 %copy.12 = bf16[1,128,2,1024]{1,3,2,0:T(8,128)(2,1)S(1)} copy(bf16[1,128,2,1024]{3,2,1,0:T(2,128)(2,1)} %param.9) | data formatting | bytes 1048576 | tf_op args[1]
  2.7 0.0 copy-start
  2.7 0.0 copy-start.1
  2.7 0.0 copy-start.2
  2.7 0.3 copy.13
  3.0 0.0 copy-start.4
  3.0 0.0 copy-start.5
  3.1 0.0 copy-done.3
  3.1 0.7 %copy-done = bf16[1,2,8,2,64,128]{5,4,3,2,1,0:T(8,128)(2,1)S(1)} copy-done((bf16[1,2,8,2,64,128]{5,4,3,2,1,0:T(8,128)(2,1)S(1)}, bf16[1,2,8,2,64,128]{5,4,3,2,1,0:T(8,128)(2,1)}, u32[]{:S(2)}) %copy-start) | copy-done | bytes 524312
  3.7 0.1 copy-done.1
  3.8 0.1 copy-done.2
  3.9 0.0 copy-done.4
  3.9 0.0 copy-done.5
  3.9 31.5 %shard_map.111 = (bf16[128,1024]{1,0:T(8,128)(2,1)S(1)}, bf16[128,1024]{1,0:T(8,128)(2,1)S(1)}, bf16[128,2,1024]{2,1,0:T(2,128)(2,1)S(1)}, f32[1,128]{1,0:T(1,128)S(1)}) custom-call(bf16[128,1024]{1,0:T(8,128)(2,1)S(1)} %bitcast.13, bf16[128,1024]{1,0:T(8,128)(2,1)S(1)} %bitcast.14, bf16[8,2,128,128]{3,2,1,0:T(8,128)(2,1)S(1)} %bitcast.10, ...), custom_call_target="tpu_custom_call" | custom-call | tf_op jit(solution)/shard_map/pallas_call | solution.py:562
  35.4 0.5 %slice_bitcast_fusion = f32[8]{0:T(128)} fusion(f32[1,128]{1,0:T(1,128)S(1)} %get-tuple-element.11), kind=kLoop, calls=%fused_computation | loop fusion | bytes 64 | tf_op jit(solution)/shard_map/squeeze | solution.py:606
  35.9 0.7 %copy.18 = bf16[1,128,1024]{2,1,0:T(8,128)(2,1)} copy(bf16[1,128,1024]{2,1,0:T(8,128)(2,1)S(1)} %bitcast.16) | data formatting | bytes 524288
  36.6 0.7 %copy.19 = bf16[1,128,1024]{2,1,0:T(8,128)(2,1)} copy(bf16[1,128,1024]{2,1,0:T(8,128)(2,1)S(1)} %bitcast.15) | data formatting | bytes 524288
  37.3 0.8 %copy.20 = bf16[1,128,2,1024]{3,2,1,0:T(2,128)(2,1)} copy(bf16[1,128,2,1024]{3,2,1,0:T(2,128)(2,1)S(1)} %bitcast.12) | data formatting | bytes 1048576
Async XLA Ops:
  1.3 1.8 %copy-start.3 = (s32[1,1,8,16]{3,2,1,0:T(8,128)S(1)}, s32[1,1,8,16]{3,2,1,0:T(8,128)}, u32[]{:S(2)}) copy-start(s32[1,1,8,16]{3,2,1,0:T(8,128)} %ids_ref.1) | copy-start | bytes 1540
  2.7 1.0 %copy-start = (bf16[1,2,8,2,64,128]{5,4,3,2,1,0:T(8,128)(2,1)S(1)}, bf16[1,2,8,2,64,128]{5,4,3,2,1,0:T(8,128)(2,1)}, u32[]{:S(2)}) copy-start(bf16[1,2,8,2,64,128]{5,4,3,2,1,0:T(8,128)(2,1)} %param.10) | copy-start | bytes 1572868
  2.7 1.1 %copy-start.1 = (bf16[1,128,1024]{2,1,0:T(8,128)(2,1)S(1)}, bf16[1,128,1024]{2,1,0:T(8,128)(2,1)}, u32[]{:S(2)}) copy-start(bf16[1,128,1024]{2,1,0:T(8,128)(2,1)} %param.8) | copy-start | bytes 786436
  2.7 1.2 %copy-start.2 = (bf16[1,128,1024]{2,1,0:T(8,128)(2,1)S(1)}, bf16[1,128,1024]{2,1,0:T(8,128)(2,1)}, u32[]{:S(2)}) copy-start(bf16[1,128,1024]{2,1,0:T(8,128)(2,1)} %param.15) | copy-start | bytes 786436
  3.0 0.9 %copy-start.4 = (s32[1,8]{1,0:T(1,128)S(1)}, s32[1,8]{1,0:T(1,128)}, u32[]{:S(2)}) copy-start(s32[1,8]{1,0:T(1,128)} %home_ref.1) | copy-start | bytes 100
  3.0 0.9 %copy-start.5 = (f32[8]{0:T(128)S(1)}, f32[8]{0:T(128)}, u32[]{:S(2)}) copy-start(f32[8]{0:T(128)} %bias_ref.1) | copy-start | bytes 100

commit v4 on v3

--- a/solution.py
+++ b/solution.py
@@ -192,7 +192,7 @@
 
 def probs_of(scores):
     top = jnp.max(scores, axis=1, keepdims=True)
-    lifted = jnp.exp(scores - top)
+    lifted = jnp.exp2((scores - top) * (SCALE * 1.4426950408889634))
     return lifted * (1.0 / jnp.sum(lifted, axis=1, keepdims=True))
 
 
@@ -427,11 +427,11 @@
         ]
         mem_keys = jnp.concatenate([entry[0] for entry in entries], axis=0)
         mem_vals = jnp.concatenate([entry[1] for entry in entries], axis=0)
-        mem_probs = probs_of(dot_nt(query, mem_keys) * SCALE + mask_s[pl.ds(head, 1), :])
+        mem_probs = probs_of(dot_nt(query, mem_keys) + mask_s[pl.ds(head, 1), :])
         mem_out = dot_nn(mem_probs.astype(bf), mem_vals)
         mem_delta = jnp.sum(mem_cot * mem_out, axis=1, keepdims=True)
         mem_ds = (
-            mem_probs * ((dot_nt(mem_cot.astype(bf), mem_vals) - mem_delta) * SCALE)
+            mem_probs * (dot_nt((mem_cot * SCALE).astype(bf), mem_vals) - mem_delta * SCALE)
         ).astype(bf)
         query_grad = dot_nn(mem_ds, mem_keys)
 
@@ -449,7 +449,7 @@
         col = lax.broadcasted_iota(jnp.int32, (rows, keys_n), 1)
         causal = col <= row + (keys_n - rows)
         near_probs = probs_of(
-            jnp.where(causal, dot_nt(query, near_keys) * SCALE, neg_large)
+            jnp.where(causal, dot_nt(query, near_keys), neg_large)
         )
         near_low = near_probs.astype(bf)
         near_out = dot_nn(near_low, near_vals)
@@ -461,7 +461,7 @@
                 copy.start()
         near_delta = jnp.sum(near_cot * near_out, axis=1, keepdims=True)
         near_ds = (
-            near_probs * ((dot_nt(near_cot16, near_vals) - near_delta) * SCALE)
+            near_probs * (dot_nt((near_cot * SCALE).astype(bf), near_vals) - near_delta * SCALE)
         ).astype(bf)
         key_grad = dot_tn(near_ds, query).astype(bf)
         val_grad = dot_tn(near_low, near_cot16).astype(bf)

time: 38.2 us -> 38.2 us (level)
  no operation moved by 1% of the time
where the time goes in v4:
time: 38.2 us; the launch traced here: 38.1 us
  Pallas kernels  31.5 us (82%)
  local copies, waits for them, and re-layouts  5.26 us (14%)
  between operations  1.36 us (4%)
    pallas_call x1, Pallas kernels, one_stretch_per_document(): pl.pallas_call(functools.partial(layer_kernel, n_dp), out_shape=(jax.Shap...  31.5 us
    unnamed x16, local copies, waits for them, and re-layouts  4.46 us

profile of v4, /device:TPU:0, one launch (start us, length us, event | category | flops | bytes accessed | tf_op | source)
XLA Modules:
  0.0 38.1 jit_solution(10420376601462176896)
XLA Ops:
  1.3 0.0 copy-start.3
  1.3 1.4 %copy.12 = bf16[1,128,2,1024]{1,3,2,0:T(8,128)(2,1)S(1)} copy(bf16[1,128,2,1024]{3,2,1,0:T(2,128)(2,1)} %param.9) | data formatting | bytes 1048576 | tf_op args[1]
  2.7 0.0 copy-start
  2.7 0.0 copy-start.1
  2.7 0.0 copy-start.2
  2.7 0.3 copy.13
  3.0 0.0 copy-start.4
  3.0 0.0 copy-start.5
  3.1 0.0 copy-done.3
  3.1 0.7 %copy-done = bf16[1,2,8,2,64,128]{5,4,3,2,1,0:T(8,128)(2,1)S(1)} copy-done((bf16[1,2,8,2,64,128]{5,4,3,2,1,0:T(8,128)(2,1)S(1)}, bf16[1,2,8,2,64,128]{5,4,3,2,1,0:T(8,128)(2,1)}, u32[]{:S(2)}) %copy-start) | copy-done | bytes 524312
  3.7 0.1 copy-done.1
  3.8 0.1 copy-done.2
  3.9 0.0 copy-done.4
  3.9 0.0 copy-done.5
  3.9 31.5 %shard_map.111 = (bf16[128,1024]{1,0:T(8,128)(2,1)S(1)}, bf16[128,1024]{1,0:T(8,128)(2,1)S(1)}, bf16[128,2,1024]{2,1,0:T(2,128)(2,1)S(1)}, f32[1,128]{1,0:T(1,128)S(1)}) custom-call(bf16[128,1024]{1,0:T(8,128)(2,1)S(1)} %bitcast.13, bf16[128,1024]{1,0:T(8,128)(2,1)S(1)} %bitcast.14, bf16[8,2,128,128]{3,2,1,0:T(8,128)(2,1)S(1)} %bitcast.10, ...), custom_call_target="tpu_custom_call" | custom-call | tf_op jit(solution)/shard_map/pallas_call | solution.py:562
  35.4 0.5 %slice_bitcast_fusion = f32[8]{0:T(128)} fusion(f32[1,128]{1,0:T(1,128)S(1)} %get-tuple-element.11), kind=kLoop, calls=%fused_computation | loop fusion | bytes 64 | tf_op jit(solution)/shard_map/squeeze | solution.py:606
  35.9 0.7 %copy.18 = bf16[1,128,1024]{2,1,0:T(8,128)(2,1)} copy(bf16[1,128,1024]{2,1,0:T(8,128)(2,1)S(1)} %bitcast.16) | data formatting | bytes 524288
  36.6 0.7 %copy.19 = bf16[1,128,1024]{2,1,0:T(8,128)(2,1)} copy(bf16[1,128,1024]{2,1,0:T(8,128)(2,1)S(1)} %bitcast.15) | data formatting | bytes 524288
  37.3 0.8 %copy.20 = bf16[1,128,2,1024]{3,2,1,0:T(2,128)(2,1)} copy(bf16[1,128,2,1024]{3,2,1,0:T(2,128)(2,1)S(1)} %bitcast.12) | data formatting | bytes 1048576
Async XLA Ops:
  1.3 1.8 %copy-start.3 = (s32[1,1,8,16]{3,2,1,0:T(8,128)S(1)}, s32[1,1,8,16]{3,2,1,0:T(8,128)}, u32[]{:S(2)}) copy-start(s32[1,1,8,16]{3,2,1,0:T(8,128)} %ids_ref.1) | copy-start | bytes 1540
  2.7 1.0 %copy-start = (bf16[1,2,8,2,64,128]{5,4,3,2,1,0:T(8,128)(2,1)S(1)}, bf16[1,2,8,2,64,128]{5,4,3,2,1,0:T(8,128)(2,1)}, u32[]{:S(2)}) copy-start(bf16[1,2,8,2,64,128]{5,4,3,2,1,0:T(8,128)(2,1)} %param.10) | copy-start | bytes 1572868
  2.7 1.1 %copy-start.1 = (bf16[1,128,1024]{2,1,0:T(8,128)(2,1)S(1)}, bf16[1,128,1024]{2,1,0:T(8,128)(2,1)}, u32[]{:S(2)}) copy-start(bf16[1,128,1024]{2,1,0:T(8,128)(2,1)} %param.8) | copy-start | bytes 786436
  2.7 1.2 %copy-start.2 = (bf16[1,128,1024]{2,1,0:T(8,128)(2,1)S(1)}, bf16[1,128,1024]{2,1,0:T(8,128)(2,1)}, u32[]{:S(2)}) copy-start(bf16[1,128,1024]{2,1,0:T(8,128)(2,1)} %param.15) | copy-start | bytes 786436
  3.0 0.9 %copy-start.4 = (s32[1,8]{1,0:T(1,128)S(1)}, s32[1,8]{1,0:T(1,128)}, u32[]{:S(2)}) copy-start(s32[1,8]{1,0:T(1,128)} %home_ref.1) | copy-start | bytes 100
  3.0 0.9 %copy-start.5 = (f32[8]{0:T(128)S(1)}, f32[8]{0:T(128)}, u32[]{:S(2)}) copy-start(f32[8]{0:T(128)} %bias_ref.1) | copy-start | bytes 100
